TPU v7x, 32 devices: a whole 2x2x4 slice. The times are simulated.
32 devices in a mesh: epoch: 16 (over z, x, core), depth: 2 (over y).
Axes of the slice: x: 2, y: 2, z: 4, core: 2. Of those that a mesh axis runs over, the one named last changes fastest.
Arguments:
- slip: bfloat16 [16, 2, 3, 8, 1024], P('epoch', 'depth'), may hold values from -6 to 6
- kernels: float32 [2, 16, 2, 3, 1024], P(None, None, 'depth'), may hold values from -0.07 to 0.07
- lag_index: int32 [16], replicated, may hold values from 0 to 15
- observed: float32 [16, 8, 1024], P('epoch', None, 'depth'), may hold values from -6 to 6
- mask: int32 [16, 8, 1024], P('epoch', None, 'depth'), may hold values 0 or 1
- noise_var: float32 [16], P('epoch'), may hold values from 0.5 to 2
- prior_prec: float32 [2, 3], P('depth'), may hold values from 0.25 to 4
Outputs:
- gradient: float32 [16, 2, 3, 8, 1024], P('epoch', 'depth')
- predicted: float32 [16, 8, 1024], P('epoch', None, 'depth')
All inputs are finite; a program needn't handle non-finite values. No bound on the sum of `mask` on one device may be relied on, other than what follows from the above.
Results may differ from a plain program's by a relative error of at most 0.0029.
Values may be sent and summed in bfloat16 or wider, within the bound.
A program may use at most 64 MiB of HBM per device.

v0:
```python
import functools
import math

import jax
import jax.numpy as jnp
import ml_dtypes
import numpy as np
from jax import lax
from jax.experimental import pallas as pl
from jax.experimental.pallas import tpu as pltpu
from jax.sharding import PartitionSpec as P

LANES = 128
PAIR = 2


def tables(columns):
    half = columns // 2
    x = np.arange(columns, dtype=np.int64)
    angle = 2.0 * math.pi * ((x[:, None] * x[None, :half]) % columns) / columns
    low = np.cos(angle)
    high = -np.sin(angle)
    high[:, 0] = 1.0 - 2.0 * (x % 2)
    forward = np.concatenate([low, high], axis=1)
    scale = np.full((columns,), 2.0 / columns)
    scale[0] = scale[half] = 1.0 / columns
    inverse = (forward * scale[None, :]).T

    def split(table):
        table = table.astype(np.float32)
        top = table.astype(ml_dtypes.bfloat16)
        rest = (table - top.astype(np.float32)).astype(ml_dtypes.bfloat16)
        return np.stack([top, rest])

    return split(forward), split(inverse)


def kernel(
    epochs, depths, owners, blocks,
    lag_ref, nv_ref, prior_ref, slip_ref, obs_ref, mask_ref, k_hbm, f_hbm, i_hbm,
    grad_ref, pred_ref,
    f_ref, i_ref, k_ref, send_a, recv_a, send_b, recv_b, send_c, recv_c, send_d, recv_d,
    send_o, recv_o, mirror, kinds_abc, lag_abc, spec, wide,
    load_sem, out_sem, in_sem,
):
    bf16, f32 = jnp.bfloat16, jnp.float32
    channels = slip_ref.shape[2]
    columns = slip_ref.shape[4]
    half = columns // 2
    kinds = k_ref.shape[1]
    width = obs_ref.shape[2]
    pairs = owners // blocks
    total = epochs * depths
    me = lax.axis_index("epoch")
    layer = lax.axis_index("depth")
    flat = me * depths + layer
    everyone_owns = epochs == owners

    load_f = pltpu.make_async_copy(f_hbm, f_ref, load_sem.at[0])
    load_i = pltpu.make_async_copy(i_hbm, i_ref, load_sem.at[1])
    load_k = pltpu.make_async_copy(k_hbm, k_ref, load_sem.at[2])
    load_f.start()
    load_k.start()
    load_i.start()

    barrier = pltpu.get_barrier_semaphore()

    @pl.loop(1, total)
    def _(step):
        other = (flat + step) % total
        pl.semaphore_signal(
            barrier, inc=1, device_id=(other // depths, other % depths),
            device_id_type=pl.DeviceIdType.MESH,
        )

    def remote(src, dst, number, epoch, depth):
        pltpu.make_async_remote_copy(
            src_ref=src, dst_ref=dst, send_sem=out_sem.at[number], recv_sem=in_sem.at[number],
            device_id=(epoch, depth), device_id_type=pl.DeviceIdType.MESH,
        ).start()

    def local(src, dst, number):
        pltpu.make_async_copy(src, dst, in_sem.at[number]).start()

    def wait_bytes(ref, sem):
        pltpu.make_async_copy(ref, ref, sem).wait()

    def to_owners(send, recv, number):
        if everyone_owns:
            @pl.loop(1, owners)
            def _(step):
                owner = (me + step) % owners
                remote(send.at[owner], recv.at[me], number, owner, layer)

            local(send.at[me], recv.at[me], number)
        else:
            @pl.loop(0, owners)
            def _(step):
                owner = (me + step) % owners

                @pl.when(owner != me)
                def _():
                    remote(send.at[owner], recv.at[me], number, owner, layer)

                @pl.when(owner == me)
                def _():
                    local(send.at[me], recv.at[me], number)

    def sent_to_owners(send, number):
        if everyone_owns:
            wait_bytes(send.at[pl.ds(0, owners - 1)], out_sem.at[number])
        else:
            @pl.when(me < owners)
            def _():
                wait_bytes(send.at[pl.ds(0, owners - 1)], out_sem.at[number])

            @pl.when(me >= owners)
            def _():
                wait_bytes(send, out_sem.at[number])

    def owner_part(part):
        if everyone_owns:
            part()
        else:
            pl.when(me < owners)(part)

    def forward(field):
        return jnp.dot(field, f_ref[0], preferred_element_type=f32) + jnp.dot(
            field, f_ref[1], preferred_element_type=f32
        )

    def inverse(value):
        top = value.astype(bf16)
        rest = (value - top.astype(f32)).astype(bf16)
        rows = value.shape[0]
        both = jnp.dot(jnp.concatenate([top, rest]), i_ref[0], preferred_element_type=f32)
        return (both[:rows] + both[rows:]) + jnp.dot(top, i_ref[1], preferred_element_type=f32)

    def scatter(value, send):
        for pair in range(pairs):
            for block in range(blocks):
                rows = slice(pair * 8, pair * 8 + 8)
                real = value[rows, block * LANES : (block + 1) * LANES]
                imag = value[rows, half + block * LANES : half + (block + 1) * LANES]
                send[pair * blocks + block] = jnp.concatenate([real, imag]).astype(bf16)

    send_o[0:8] = obs_ref[0]
    send_o[8:16] = mask_ref[0].astype(f32)

    padded = pairs * 8
    row = lax.broadcasted_iota(jnp.int32, (padded, channels * 8), 0)
    source = lax.broadcasted_iota(jnp.int32, (padded, channels * 8), 1)
    wanted = (row % 8) // PAIR * 8 + row // 8 * PAIR + row % PAIR
    order = ((wanted == source) & (row % 8 < channels * PAIR)).astype(bf16)
    slip_rows = jnp.concatenate([slip_ref[0, 0, c].astype(f32) for c in range(channels)])
    slip_wide = jnp.dot(order, slip_rows.astype(bf16), preferred_element_type=f32)

    load_f.wait()
    scatter(forward(slip_wide.astype(bf16)), send_a)
    pl.semaphore_wait(barrier, total - 1)
    to_owners(send_a, recv_a, 0)

    @pl.loop(1, depths)
    def _(step):
        remote(send_o, recv_o.at[layer], 4, me, (layer + step) % depths)

    local(send_o, recv_o.at[layer], 4)

    load_k.wait()

    def prepare():
        block = me % blocks
        row8 = lax.broadcasted_iota(jnp.int32, (8, LANES), 0)
        lane = lax.broadcasted_iota(jnp.int32, (8, LANES), 1)

        def tile(part, kind, place):
            lanes = pl.ds(pl.multiple_of(place * LANES, LANES), LANES)
            value = k_ref[part, kind, 0, :, lanes]
            out = jnp.zeros((8, LANES), f32)
            for c in range(channels):
                out = jnp.where(row8 // PAIR == c, value[c : c + 1], out)
            return out

        count = 2 * blocks

        @pl.loop(0, kinds)
        def _(kind):
            for part in range(2):
                mirror[part, kind] = tile(part, kind, count - 1 - block)

        j = lax.broadcasted_iota(jnp.int32, (LANES, LANES), 0)
        i = lax.broadcasted_iota(jnp.int32, (LANES, LANES), 1)
        turn = (i + j == LANES).astype(f32)
        turned = jnp.dot(
            mirror[...].reshape(2 * kinds * 8, LANES), turn,
            precision=lax.Precision.HIGHEST, preferred_element_type=f32,
        )
        mirror[...] = turned.reshape(2, kinds, 8, LANES)

        @pl.loop(0, kinds)
        def _(kind):
            first = (count - block) % count
            real = jnp.where(lane == 0, tile(0, kind, first), mirror[0, kind])
            imag = jnp.where(lane == 0, tile(1, kind, first), mirror[1, kind])
            real = 0.5 * (tile(0, kind, block) + real)
            imag = 0.5 * (tile(1, kind, block) - imag)
            middle = tile(0, kind, blocks)
            kinds_abc[kind, 0] = real
            kinds_abc[kind, 1] = imag
            kinds_abc[kind, 2] = jnp.where((lane == 0) & (block == 0), middle, real)

        lag_abc[pl.ds(0, epochs)] = jnp.zeros((epochs, 3, 8, LANES), f32)

        @pl.loop(0, epochs)
        def _(lag):
            lag_abc[epochs + lag] = kinds_abc[lag_ref[lag]]

    owner_part(prepare)

    def unpack(recv):
        @pl.loop(0, epochs)
        def _(epoch):
            value = recv[epoch].astype(f32)
            spec[epoch, 0] = value[0:8]
            spec[epoch, 1] = value[8:16]

    row8 = lax.broadcasted_iota(jnp.int32, (8, LANES), 0)

    def predict():
        wait_bytes(recv_a, in_sem.at[0])
        unpack(recv_a)

        @pl.loop(0, epochs)
        def _(target):
            real = jnp.zeros((8, LANES), f32)
            imag = jnp.zeros((8, LANES), f32)
            for s in range(epochs):
                at = epochs + target - s
                a, b, c = lag_abc[at, 0], lag_abc[at, 1], lag_abc[at, 2]
                sr, si = spec[s, 0], spec[s, 1]
                real = real + (a * sr - b * si)
                imag = imag + (c * si + b * sr)
            real = real + pltpu.roll(real, 4, 0)
            real = real + pltpu.roll(real, 2, 0)
            imag = imag + pltpu.roll(imag, 4, 0)
            imag = imag + pltpu.roll(imag, 2, 0)
            send_b[target] = jnp.where(row8 < 4, real, imag)

        @pl.loop(1, total)
        def _(step):
            other = (flat + step) % total
            epoch = other // depths
            remote(send_b.at[epoch], recv_b.at[layer, me], 1, epoch, other % depths)

        local(send_b.at[me], recv_b.at[layer, me], 1)

    owner_part(predict)

    wait_bytes(recv_o, in_sem.at[4])
    inv = 1.0 / jnp.full((8, columns), nv_ref[0], f32)
    seen = jnp.concatenate([recv_o[d, 0:8] for d in range(depths)], axis=1)
    weight = jnp.concatenate([recv_o[d, 8:16] for d in range(depths)], axis=1) * inv
    rowp = lax.broadcasted_iota(jnp.int32, (padded, 8), 0)
    colp = lax.broadcasted_iota(jnp.int32, (padded, 8), 1)
    spread = (rowp // 8 * PAIR + rowp % PAIR == colp).astype(f32)
    seen_wide = jnp.dot(
        spread, seen, precision=lax.Precision.HIGHEST, preferred_element_type=f32
    )
    weight_wide = jnp.dot(
        spread, weight, precision=lax.Precision.HIGHEST, preferred_element_type=f32
    )
    load_i.wait()

    wait_bytes(recv_b, in_sem.at[1])
    for pair in range(pairs):
        for block in range(blocks):
            value = recv_b[0, pair * blocks + block]
            for d in range(1, depths):
                value = value + recv_b[d, pair * blocks + block]
            turned = pltpu.roll(value, 4, 0)
            rows = slice(pair * 8, pair * 8 + 8)
            wide[rows, block * LANES : (block + 1) * LANES] = jnp.where(row8 < 4, value, turned)
            wide[rows, half + block * LANES : half + (block + 1) * LANES] = jnp.where(
                row8 < 4, turned, value
            )
    predicted = inverse(wide[...])
    resid = (weight_wide * (predicted - seen_wide)).astype(bf16)
    scatter(forward(resid), send_c)
    to_owners(send_c, recv_c, 2)

    wide[...] = predicted
    mine = pl.ds(pl.multiple_of(layer * width, LANES), width)
    for pair in range(pairs):
        pred_ref[0, pair * PAIR : (pair + 1) * PAIR, :] = wide[pair * 8 : pair * 8 + PAIR, mine]

    def adjoint():
        wait_bytes(recv_c, in_sem.at[2])
        unpack(recv_c)

        @pl.loop(0, epochs)
        def _(origin):
            real = jnp.zeros((8, LANES), f32)
            imag = jnp.zeros((8, LANES), f32)
            for t in range(epochs):
                at = epochs + t - origin
                a, b, c = lag_abc[at, 0], lag_abc[at, 1], lag_abc[at, 2]
                qr, qi = spec[t, 0], spec[t, 1]
                real = real + (a * qr + b * qi)
                imag = imag + (c * qi - b * qr)
            send_d[origin, 0:8] = real
            send_d[origin, 8:16] = imag

        @pl.loop(1, epochs)
        def _(step):
            epoch = (me + step) % epochs
            remote(send_d.at[epoch], recv_d.at[me], 3, epoch, layer)

        local(send_d.at[me], recv_d.at[me], 3)

    owner_part(adjoint)

    rowc = lax.broadcasted_iota(jnp.int32, (padded, columns), 0) % 8 // PAIR
    prior = jnp.zeros((padded, columns), f32)
    for c in range(channels):
        prior = jnp.where(rowc == c, prior_ref[0, c], prior)
    prior = prior * slip_wide

    wait_bytes(recv_d, in_sem.at[3])
    for pair in range(pairs):
        for block in range(blocks):
            rows = slice(pair * 8, pair * 8 + 8)
            wide[rows, block * LANES : (block + 1) * LANES] = recv_d[pair * blocks + block, 0:8]
            wide[rows, half + block * LANES : half + (block + 1) * LANES] = recv_d[
                pair * blocks + block, 8:16
            ]
    result = -inverse(wide[...]) - prior
    for pair in range(pairs):
        for c in range(channels):
            first = pair * 8 + c * PAIR
            grad_ref[0, 0, c, pair * PAIR : (pair + 1) * PAIR, :] = result[first : first + PAIR]

    sent_to_owners(send_a, 0)
    sent_to_owners(send_c, 2)

    def sent():
        @pl.loop(1, total)
        def _(step):
            wait_bytes(send_b.at[0], out_sem.at[1])

        wait_bytes(send_d.at[pl.ds(0, epochs - 1)], out_sem.at[3])

    owner_part(sent)

    @pl.loop(1, depths)
    def _(step):
        wait_bytes(send_o, out_sem.at[4])


def body(epochs, depths, slip, kernels, lag_index, observed, mask, noise_var, prior_prec):
    columns = slip.shape[-1]
    channels = slip.shape[2]
    kinds = kernels.shape[1]
    rows = slip.shape[3]
    blocks = columns // 2 // LANES
    owners = blocks * rows // PAIR
    padded = rows // PAIR * 8
    forward_table, inverse_table = tables(columns)
    f32, bf16 = jnp.float32, jnp.bfloat16
    vmem = pl.BlockSpec(memory_space=pltpu.VMEM)
    smem = pl.BlockSpec(memory_space=pltpu.SMEM)
    hbm = pl.BlockSpec(memory_space=pl.ANY)
    return pl.pallas_call(
        functools.partial(kernel, epochs, depths, owners, blocks),
        out_shape=(
            jax.ShapeDtypeStruct(slip.shape, f32),
            jax.ShapeDtypeStruct(observed.shape, f32),
        ),
        in_specs=[smem, smem, smem, vmem, vmem, vmem, hbm, hbm, hbm],
        out_specs=(vmem, vmem),
        scratch_shapes=[
            pltpu.VMEM((2, columns, columns), bf16),
            pltpu.VMEM((2, columns, columns), bf16),
            pltpu.VMEM(kernels.shape, f32),
            pltpu.VMEM((owners, 16, LANES), bf16),
            pltpu.VMEM((epochs, 16, LANES), bf16),
            pltpu.VMEM((epochs, 8, LANES), f32),
            pltpu.VMEM((depths, owners, 8, LANES), f32),
            pltpu.VMEM((owners, 16, LANES), bf16),
            pltpu.VMEM((epochs, 16, LANES), bf16),
            pltpu.VMEM((epochs, 16, LANES), f32),
            pltpu.VMEM((owners, 16, LANES), f32),
            pltpu.VMEM((16, observed.shape[2]), f32),
            pltpu.VMEM((depths, 16, observed.shape[2]), f32),
            pltpu.VMEM((2, kinds, 8, LANES), f32),
            pltpu.VMEM((kinds, 3, 8, LANES), f32),
            pltpu.VMEM((2 * epochs, 3, 8, LANES), f32),
            pltpu.VMEM((epochs, 2, 8, LANES), f32),
            pltpu.VMEM((padded, columns), f32),
            pltpu.SemaphoreType.DMA((3,)),
            pltpu.SemaphoreType.DMA((5,)),
            pltpu.SemaphoreType.DMA((5,)),
        ],
        compiler_params=pltpu.CompilerParams(
            collective_id=0, has_side_effects=True, vmem_limit_bytes=40 * 1024 * 1024
        ),
    )(
        lag_index, noise_var, prior_prec, slip, observed, mask, kernels,
        jnp.asarray(forward_table), jnp.asarray(inverse_table),
    )


def solution(mesh):
    in_specs = (
        P("epoch", "depth", None, None, None),
        P(None, None, "depth", None, None),
        P(),
        P("epoch", None, "depth"),
        P("epoch", None, "depth"),
        P("epoch"),
        P("depth", None),
    )
    out_specs = (P("epoch", "depth", None, None, None), P("epoch", None, "depth"))
    run = functools.partial(body, mesh.shape["epoch"], mesh.shape["depth"])
    return jax.shard_map(run, mesh=mesh, in_specs=in_specs, out_specs=out_specs, check_vma=False)
```

profile of v0, /device:TPU:0, one launch (start us, length us, event | category | flops | bytes accessed | tf_op | source)
XLA Modules:
  0.0 40.6 jit_solution(12467691793553299540)
XLA Ops:
  1.3 1.1 %copy.11.k_hbm = f32[2,16,1,3,1024]{4,3,2,1,0:T(4,128)S(1)} copy(f32[2,16,1,3,1024]{4,2,3,1,0:T(1,128)} %param.10) | data formatting | bytes 786432 | tf_op args[1]
  2.4 0.0 copy-start
  2.4 2.2 %copy-done = bf16[2,1024,1024]{2,1,0:T(8,128)(2,1)S(1)} copy-done((bf16[2,1024,1024]{2,1,0:T(8,128)(2,1)S(1)}, bf16[2,1024,1024]{2,1,0:T(8,128)(2,1)}, u32[]{:S(2)}) %copy-start) | copy-done | bytes 4194328
  4.6 0.0 copy-start.1
  4.6 2.2 %copy-done.1 = bf16[2,1024,1024]{2,1,0:T(8,128)(2,1)S(1)} copy-done((bf16[2,1024,1024]{2,1,0:T(8,128)(2,1)S(1)}, bf16[2,1024,1024]{2,1,0:T(8,128)(2,1)}, u32[]{:S(2)}) %copy-start.1) | copy-done | bytes 4194328
  6.8 0.0 copy-start.2
  6.8 0.8 %copy-done.2 = bf16[1,1,3,8,1024]{4,3,2,1,0:T(8,128)(2,1)S(1)} copy-done((bf16[1,1,3,8,1024]{4,3,2,1,0:T(8,128)(2,1)S(1)}, bf16[1,1,3,8,1024]{4,3,2,1,0:T(8,128)(2,1)}, u32[]{:S(2)}) %copy-start.2) | copy-done | bytes 49176
  7.6 0.0 copy-start.3
  7.6 0.7 %copy-done.3 = f32[1,8,512]{2,1,0:T(8,128)S(1)} copy-done((f32[1,8,512]{2,1,0:T(8,128)S(1)}, f32[1,8,512]{2,1,0:T(8,128)}, u32[]{:S(2)}) %copy-start.3) | copy-done | bytes 16408
  8.3 0.0 copy-start.4
  8.3 0.7 %copy-done.4 = s32[1,8,512]{2,1,0:T(8,128)S(1)} copy-done((s32[1,8,512]{2,1,0:T(8,128)S(1)}, s32[1,8,512]{2,1,0:T(8,128)}, u32[]{:S(2)}) %copy-start.4) | copy-done | bytes 16408
  9.0 0.0 copy-start.5
  9.0 0.7 %copy-done.5 = s32[16]{0:T(128)S(1)} copy-done((s32[16]{0:T(128)S(1)}, s32[16]{0:T(128)}, u32[]{:S(2)}) %copy-start.5) | copy-done | bytes 88
  9.7 0.0 copy-start.6
  9.7 0.7 %copy-done.6 = f32[1,3]{1,0:T(1,128)S(1)} copy-done((f32[1,3]{1,0:T(1,128)S(1)}, f32[1,3]{1,0:T(1,128)}, u32[]{:S(2)}) %copy-start.6) | copy-done | bytes 36
  10.3 29.0 %shard_map.104 = (f32[1,1,3,8,1024]{4,3,2,1,0:T(8,128)S(1)}, f32[1,8,512]{2,1,0:T(8,128)S(1)}) custom-call(s32[16]{0:T(128)S(1)} %copy-done.5, f32[1]{0:T(128)S(6)} %copy.14.nv_ref, f32[1,3]{1,0:T(1,128)S(1)} %copy-done.6, bf16[1,1,3,8,1024]{4,3,2,1,0:T(8,128)(2,1)S(1)} %copy-done.2, f32[1,8,512]{2,1,0:T(8,128)S(1)} %copy-done.3, ...), custom_call_target="tpu_custom_call" | custom-call | tf_op jit(solution)/shard_map/pallas_call | solution.py:372
  39.3 0.6 %copy.15 = f32[1,1,3,8,1024]{4,3,2,1,0:T(8,128)} copy(f32[1,1,3,8,1024]{4,3,2,1,0:T(8,128)S(1)} %get-tuple-element.4) | data formatting | bytes 196608
  40.0 0.6 %copy.16 = f32[1,8,512]{2,1,0:T(8,128)} copy(f32[1,8,512]{2,1,0:T(8,128)S(1)} %get-tuple-element.5) | data formatting | bytes 32768
Async XLA Ops:
  2.4 2.2 %copy-start = (bf16[2,1024,1024]{2,1,0:T(8,128)(2,1)S(1)}, bf16[2,1024,1024]{2,1,0:T(8,128)(2,1)}, u32[]{:S(2)}) copy-start(bf16[2,1024,1024]{2,1,0:T(8,128)(2,1)} %constant.5.clone.i_hbm) | copy-start | bytes 12582916
  4.6 2.2 %copy-start.1 = (bf16[2,1024,1024]{2,1,0:T(8,128)(2,1)S(1)}, bf16[2,1024,1024]{2,1,0:T(8,128)(2,1)}, u32[]{:S(2)}) copy-start(bf16[2,1024,1024]{2,1,0:T(8,128)(2,1)} %constant.4.clone.f_hbm) | copy-start | bytes 12582916
  6.8 0.8 %copy-start.2 = (bf16[1,1,3,8,1024]{4,3,2,1,0:T(8,128)(2,1)S(1)}, bf16[1,1,3,8,1024]{4,3,2,1,0:T(8,128)(2,1)}, u32[]{:S(2)}) copy-start(bf16[1,1,3,8,1024]{4,3,2,1,0:T(8,128)(2,1)} %slip_ref.1) | copy-start | bytes 147460
  7.6 0.7 %copy-start.3 = (f32[1,8,512]{2,1,0:T(8,128)S(1)}, f32[1,8,512]{2,1,0:T(8,128)}, u32[]{:S(2)}) copy-start(f32[1,8,512]{2,1,0:T(8,128)} %obs_ref.1) | copy-start | bytes 49156
  8.3 0.7 %copy-start.4 = (s32[1,8,512]{2,1,0:T(8,128)S(1)}, s32[1,8,512]{2,1,0:T(8,128)}, u32[]{:S(2)}) copy-start(s32[1,8,512]{2,1,0:T(8,128)} %mask_ref.1) | copy-start | bytes 49156
  9.0 0.7 %copy-start.5 = (s32[16]{0:T(128)S(1)}, s32[16]{0:T(128)}, u32[]{:S(2)}) copy-start(s32[16]{0:T(128)} %lag_ref.1) | copy-start | bytes 196
  9.7 0.7 %copy-start.6 = (f32[1,3]{1,0:T(1,128)S(1)}, f32[1,3]{1,0:T(1,128)}, u32[]{:S(2)}) copy-start(f32[1,3]{1,0:T(1,128)} %prior_ref.1) | copy-start | bytes 40
where the time goes:
time: 41 us; the launch traced here: 40.6 us
  Pallas kernels  29 us (71%)
  local copies, waits for them, and re-layouts  10.3 us (25%)
  between operations  1.31 us (3%)
    pallas_call x1, Pallas kernels, body(): pl.pallas_call(functools.partial(kernel, epochs, depths, owners, blocks),...  29 us
    unnamed x17, local copies, waits for them, and re-layouts  10.3 us

commit v1 on v0

--- a/solution.py
+++ b/solution.py
@@ -37,9 +37,9 @@
 
 def kernel(
     epochs, depths, owners, blocks,
-    lag_ref, nv_ref, prior_ref, slip_ref, obs_ref, mask_ref, k_hbm, f_hbm, i_hbm,
+    lag_ref, nv_ref, prior_ref, slip_hbm, obs_hbm, mask_hbm, k_hbm, f_hbm, i_hbm,
     grad_ref, pred_ref,
-    f_ref, i_ref, k_ref, send_a, recv_a, send_b, recv_b, send_c, recv_c, send_d, recv_d,
+    slip_ref, obs_ref, mask_ref, f_ref, i_ref, k_ref, send_a, recv_a, send_b, recv_b, send_c, recv_c, send_d, recv_d,
     send_o, recv_o, mirror, kinds_abc, lag_abc, spec, wide,
     load_sem, out_sem, in_sem,
 ):
@@ -59,8 +59,14 @@
     load_f = pltpu.make_async_copy(f_hbm, f_ref, load_sem.at[0])
     load_i = pltpu.make_async_copy(i_hbm, i_ref, load_sem.at[1])
     load_k = pltpu.make_async_copy(k_hbm, k_ref, load_sem.at[2])
+    load_s = pltpu.make_async_copy(slip_hbm, slip_ref, load_sem.at[3])
+    load_o = pltpu.make_async_copy(obs_hbm, obs_ref, load_sem.at[4])
+    load_m = pltpu.make_async_copy(mask_hbm, mask_ref, load_sem.at[5])
+    load_k.start()
+    load_s.start()
+    load_o.start()
+    load_m.start()
     load_f.start()
-    load_k.start()
     load_i.start()
 
     barrier = pltpu.get_barrier_semaphore()
@@ -144,28 +150,6 @@
                 imag = value[rows, half + block * LANES : half + (block + 1) * LANES]
                 send[pair * blocks + block] = jnp.concatenate([real, imag]).astype(bf16)
 
-    send_o[0:8] = obs_ref[0]
-    send_o[8:16] = mask_ref[0].astype(f32)
-
-    padded = pairs * 8
-    row = lax.broadcasted_iota(jnp.int32, (padded, channels * 8), 0)
-    source = lax.broadcasted_iota(jnp.int32, (padded, channels * 8), 1)
-    wanted = (row % 8) // PAIR * 8 + row // 8 * PAIR + row % PAIR
-    order = ((wanted == source) & (row % 8 < channels * PAIR)).astype(bf16)
-    slip_rows = jnp.concatenate([slip_ref[0, 0, c].astype(f32) for c in range(channels)])
-    slip_wide = jnp.dot(order, slip_rows.astype(bf16), preferred_element_type=f32)
-
-    load_f.wait()
-    scatter(forward(slip_wide.astype(bf16)), send_a)
-    pl.semaphore_wait(barrier, total - 1)
-    to_owners(send_a, recv_a, 0)
-
-    @pl.loop(1, depths)
-    def _(step):
-        remote(send_o, recv_o.at[layer], 4, me, (layer + step) % depths)
-
-    local(send_o, recv_o.at[layer], 4)
-
     load_k.wait()
 
     def prepare():
@@ -175,10 +159,9 @@
 
         def tile(part, kind, place):
             lanes = pl.ds(pl.multiple_of(place * LANES, LANES), LANES)
-            value = k_ref[part, kind, 0, :, lanes]
             out = jnp.zeros((8, LANES), f32)
             for c in range(channels):
-                out = jnp.where(row8 // PAIR == c, value[c : c + 1], out)
+                out = jnp.where(row8 // PAIR == c, k_ref[part, kind, c, :, lanes], out)
             return out
 
         count = 2 * blocks
@@ -217,6 +200,31 @@
 
     owner_part(prepare)
 
+    load_o.wait()
+    load_m.wait()
+    send_o[0:8] = obs_ref[0]
+    send_o[8:16] = mask_ref[0].astype(f32)
+
+    padded = pairs * 8
+    row = lax.broadcasted_iota(jnp.int32, (padded, channels * 8), 0)
+    source = lax.broadcasted_iota(jnp.int32, (padded, channels * 8), 1)
+    wanted = (row % 8) // PAIR * 8 + row // 8 * PAIR + row % PAIR
+    order = ((wanted == source) & (row % 8 < channels * PAIR)).astype(bf16)
+    load_s.wait()
+    slip_rows = jnp.concatenate([slip_ref[0, 0, c].astype(f32) for c in range(channels)])
+    slip_wide = jnp.dot(order, slip_rows.astype(bf16), preferred_element_type=f32)
+
+    load_f.wait()
+    scatter(forward(slip_wide.astype(bf16)), send_a)
+    pl.semaphore_wait(barrier, total - 1)
+    to_owners(send_a, recv_a, 0)
+
+    @pl.loop(1, depths)
+    def _(step):
+        remote(send_o, recv_o.at[layer], 4, me, (layer + step) % depths)
+
+    local(send_o, recv_o.at[layer], 4)
+
     def unpack(recv):
         @pl.loop(0, epochs)
         def _(epoch):
@@ -230,8 +238,9 @@
         wait_bytes(recv_a, in_sem.at[0])
         unpack(recv_a)
 
-        @pl.loop(0, epochs)
-        def _(target):
+        @pl.loop(1, epochs + 1)
+        def _(step):
+            target = (me + step) % epochs
             real = jnp.zeros((8, LANES), f32)
             imag = jnp.zeros((8, LANES), f32)
             for s in range(epochs):
@@ -246,11 +255,12 @@
             imag = imag + pltpu.roll(imag, 2, 0)
             send_b[target] = jnp.where(row8 < 4, real, imag)
 
-        @pl.loop(1, total)
-        def _(step):
-            other = (flat + step) % total
-            epoch = other // depths
-            remote(send_b.at[epoch], recv_b.at[layer, me], 1, epoch, other % depths)
+            for turn in range(1, depths):
+                remote(send_b.at[target], recv_b.at[layer, me], 1, target, (layer + turn) % depths)
+
+            @pl.when(step < epochs)
+            def _():
+                remote(send_b.at[target], recv_b.at[layer, me], 1, target, layer)
 
         local(send_b.at[me], recv_b.at[layer, me], 1)
 
@@ -297,8 +307,9 @@
         wait_bytes(recv_c, in_sem.at[2])
         unpack(recv_c)
 
-        @pl.loop(0, epochs)
-        def _(origin):
+        @pl.loop(1, epochs + 1)
+        def _(step):
+            origin = (me + step) % epochs
             real = jnp.zeros((8, LANES), f32)
             imag = jnp.zeros((8, LANES), f32)
             for t in range(epochs):
@@ -310,10 +321,9 @@
             send_d[origin, 0:8] = real
             send_d[origin, 8:16] = imag
 
-        @pl.loop(1, epochs)
-        def _(step):
-            epoch = (me + step) % epochs
-            remote(send_d.at[epoch], recv_d.at[me], 3, epoch, layer)
+            @pl.when(step < epochs)
+            def _():
+                remote(send_d.at[origin], recv_d.at[me], 3, origin, layer)
 
         local(send_d.at[me], recv_d.at[me], 3)
 
@@ -368,16 +378,20 @@
     f32, bf16 = jnp.float32, jnp.bfloat16
     vmem = pl.BlockSpec(memory_space=pltpu.VMEM)
     smem = pl.BlockSpec(memory_space=pltpu.SMEM)
-    hbm = pl.BlockSpec(memory_space=pl.ANY)
+    hbm = pl.BlockSpec(memory_space=pltpu.HBM)
+    kernels = jnp.swapaxes(kernels, 2, 3)
     return pl.pallas_call(
         functools.partial(kernel, epochs, depths, owners, blocks),
         out_shape=(
             jax.ShapeDtypeStruct(slip.shape, f32),
             jax.ShapeDtypeStruct(observed.shape, f32),
         ),
-        in_specs=[smem, smem, smem, vmem, vmem, vmem, hbm, hbm, hbm],
+        in_specs=[smem, smem, smem, hbm, hbm, hbm, hbm, hbm, hbm],
         out_specs=(vmem, vmem),
         scratch_shapes=[
+            pltpu.VMEM(slip.shape, bf16),
+            pltpu.VMEM(observed.shape, f32),
+            pltpu.VMEM(mask.shape, mask.dtype),
             pltpu.VMEM((2, columns, columns), bf16),
             pltpu.VMEM((2, columns, columns), bf16),
             pltpu.VMEM(kernels.shape, f32),
@@ -396,12 +410,12 @@
             pltpu.VMEM((2 * epochs, 3, 8, LANES), f32),
             pltpu.VMEM((epochs, 2, 8, LANES), f32),
             pltpu.VMEM((padded, columns), f32),
-            pltpu.SemaphoreType.DMA((3,)),
+            pltpu.SemaphoreType.DMA((6,)),
             pltpu.SemaphoreType.DMA((5,)),
             pltpu.SemaphoreType.DMA((5,)),
         ],
         compiler_params=pltpu.CompilerParams(
-            collective_id=0, has_side_effects=True, vmem_limit_bytes=40 * 1024 * 1024
+            collective_id=0, has_side_effects=True, vmem_limit_bytes=60 * 1024 * 1024
         ),
     )(
         lag_index, noise_var, prior_prec, slip, observed, mask, kernels,

time: 41 us -> 33.7 us (0.82)
  local copies, waits for them, and re-layouts: 10.3 us -> 2.86 us
    unnamed x17 -> x2, local copies, waits for them, and re-layouts: 10.3 us -> 2.86 us
where the time goes in v1:
time: 33.7 us; the launch traced here: 33.5 us
  Pallas kernels  29.3 us (87%)
  local copies, waits for them, and re-layouts  2.86 us (8%)
  between operations  1.29 us (4%)
    pallas_call x1, Pallas kernels, body(): pl.pallas_call(functools.partial(kernel, epochs, depths, owners, blocks),...  29.3 us
    unnamed x2, local copies, waits for them, and re-layouts  2.86 us

profile of v1, /device:TPU:0, one launch (start us, length us, event | category | flops | bytes accessed | tf_op | source)
XLA Modules:
  0.0 33.5 jit_solution(3442216348369575588)
XLA Ops:
  1.3 29.3 %shard_map.104 = (f32[1,1,3,8,1024]{4,3,2,1,0:T(8,128)}, f32[1,8,512]{2,1,0:T(8,128)}) custom-call(s32[16]{0:T(128)} %lag_ref.1, f32[1]{0:T(128)S(6)} %copy.13.nv_ref, f32[1,3]{1,0:T(1,128)} %prior_ref.1, bf16[1,1,3,8,1024]{4,3,2,1,0:T(8,128)(2,1)} %slip_hbm.1, f32[1,8,512]{2,1,0:T(8,128)} %obs_hbm.1, s32[1,8,512]{2,1,0:T(8,128)} %mask_hbm.1, ...), custom_call_target="tpu_custom_call" | custom-call | tf_op jit(solution)/shard_map/pallas_call | solution.py:383
  30.6 1.5 %copy.14 = f32[1,1,3,8,1024]{4,3,2,1,0:T(8,128)} copy(f32[1,1,3,8,1024]{4,3,2,1,0:T(8,128)} %get-tuple-element.4) | data formatting | bytes 196608
  32.1 1.3 %copy.15 = f32[1,8,512]{2,1,0:T(8,128)} copy(f32[1,8,512]{2,1,0:T(8,128)} %get-tuple-element.5) | data formatting | bytes 32768

commit v2 on v1

--- a/solution.py
+++ b/solution.py
@@ -253,7 +253,7 @@
             real = real + pltpu.roll(real, 2, 0)
             imag = imag + pltpu.roll(imag, 4, 0)
             imag = imag + pltpu.roll(imag, 2, 0)
-            send_b[target] = jnp.where(row8 < 4, real, imag)
+            send_b[target] = jnp.where(row8 < PAIR, real, imag)[: 2 * PAIR]
 
             for turn in range(1, depths):
                 remote(send_b.at[target], recv_b.at[layer, me], 1, target, (layer + turn) % depths)
@@ -287,11 +287,14 @@
             value = recv_b[0, pair * blocks + block]
             for d in range(1, depths):
                 value = value + recv_b[d, pair * blocks + block]
-            turned = pltpu.roll(value, 4, 0)
+            value = jnp.concatenate([value, value])
+            turned = pltpu.roll(value, PAIR, 0)
             rows = slice(pair * 8, pair * 8 + 8)
-            wide[rows, block * LANES : (block + 1) * LANES] = jnp.where(row8 < 4, value, turned)
+            wide[rows, block * LANES : (block + 1) * LANES] = jnp.where(
+                row8 % 4 < PAIR, value, turned
+            )
             wide[rows, half + block * LANES : half + (block + 1) * LANES] = jnp.where(
-                row8 < 4, turned, value
+                row8 % 4 < PAIR, turned, value
             )
     predicted = inverse(wide[...])
     resid = (weight_wide * (predicted - seen_wide)).astype(bf16)
@@ -318,8 +321,7 @@
                 qr, qi = spec[t, 0], spec[t, 1]
                 real = real + (a * qr + b * qi)
                 imag = imag + (c * qi - b * qr)
-            send_d[origin, 0:8] = real
-            send_d[origin, 8:16] = imag
+            send_d[origin] = jnp.concatenate([real, imag]).astype(bf16)
 
             @pl.when(step < epochs)
             def _():
@@ -339,11 +341,14 @@
     for pair in range(pairs):
         for block in range(blocks):
             rows = slice(pair * 8, pair * 8 + 8)
-            wide[rows, block * LANES : (block + 1) * LANES] = recv_d[pair * blocks + block, 0:8]
-            wide[rows, half + block * LANES : half + (block + 1) * LANES] = recv_d[
-                pair * blocks + block, 8:16
-            ]
-    result = -inverse(wide[...]) - prior
+            value = recv_d[pair * blocks + block].astype(f32)
+            wide[rows, block * LANES : (block + 1) * LANES] = value[0:8]
+            wide[rows, half + block * LANES : half + (block + 1) * LANES] = value[8:16]
+    held = wide[...].astype(bf16)
+    back = jnp.dot(held, i_ref[0], preferred_element_type=f32) + jnp.dot(
+        held, i_ref[1], preferred_element_type=f32
+    )
+    result = -back - prior
     for pair in range(pairs):
         for c in range(channels):
             first = pair * 8 + c * PAIR
@@ -397,12 +402,12 @@
             pltpu.VMEM(kernels.shape, f32),
             pltpu.VMEM((owners, 16, LANES), bf16),
             pltpu.VMEM((epochs, 16, LANES), bf16),
-            pltpu.VMEM((epochs, 8, LANES), f32),
-            pltpu.VMEM((depths, owners, 8, LANES), f32),
+            pltpu.VMEM((epochs, 2 * PAIR, LANES), f32),
+            pltpu.VMEM((depths, owners, 2 * PAIR, LANES), f32),
             pltpu.VMEM((owners, 16, LANES), bf16),
             pltpu.VMEM((epochs, 16, LANES), bf16),
-            pltpu.VMEM((epochs, 16, LANES), f32),
-            pltpu.VMEM((owners, 16, LANES), f32),
+            pltpu.VMEM((epochs, 16, LANES), bf16),
+            pltpu.VMEM((owners, 16, LANES), bf16),
             pltpu.VMEM((16, observed.shape[2]), f32),
             pltpu.VMEM((depths, 16, observed.shape[2]), f32),
             pltpu.VMEM((2, kinds, 8, LANES), f32),

time: 33.7 us -> 32.4 us (0.961)
  Pallas kernels: 29.3 us -> 28 us
    pallas_call x1, Pallas kernels: 29.3 us -> 28 us  [body(): pl.pallas_call(functools.partial(kernel, epochs, depths, owners, blocks),...]
where the time goes in v2:
time: 32.4 us; the launch traced here: 32.1 us
  Pallas kernels  28 us (86%)
  local copies, waits for them, and re-layouts  2.86 us (9%)
  between operations  1.29 us (4%)
    pallas_call x1, Pallas kernels, body(): pl.pallas_call(functools.partial(kernel, epochs, depths, owners, blocks),...  28 us
    unnamed x2, local copies, waits for them, and re-layouts  2.86 us

profile of v2, /device:TPU:0, one launch (start us, length us, event | category | flops | bytes accessed | tf_op | source)
XLA Modules:
  0.0 32.1 jit_solution(3083064422583565589)
XLA Ops:
  1.3 28.0 %shard_map.104 = (f32[1,1,3,8,1024]{4,3,2,1,0:T(8,128)}, f32[1,8,512]{2,1,0:T(8,128)}) custom-call(s32[16]{0:T(128)} %lag_ref.1, f32[1]{0:T(128)S(6)} %copy.13.nv_ref, f32[1,3]{1,0:T(1,128)} %prior_ref.1, bf16[1,1,3,8,1024]{4,3,2,1,0:T(8,128)(2,1)} %slip_hbm.1, f32[1,8,512]{2,1,0:T(8,128)} %obs_hbm.1, s32[1,8,512]{2,1,0:T(8,128)} %mask_hbm.1, ...), custom_call_target="tpu_custom_call" | custom-call | tf_op jit(solution)/shard_map/pallas_call | solution.py:388
  29.3 1.5 %copy.14 = f32[1,1,3,8,1024]{4,3,2,1,0:T(8,128)} copy(f32[1,1,3,8,1024]{4,3,2,1,0:T(8,128)} %get-tuple-element.4) | data formatting | bytes 196608
  30.8 1.3 %copy.15 = f32[1,8,512]{2,1,0:T(8,128)} copy(f32[1,8,512]{2,1,0:T(8,128)} %get-tuple-element.5) | data formatting | bytes 32768

commit v3 on v2

--- a/solution.py
+++ b/solution.py
@@ -91,26 +91,19 @@
     def wait_bytes(ref, sem):
         pltpu.make_async_copy(ref, ref, sem).wait()
 
-    def to_owners(send, recv, number):
-        if everyone_owns:
-            @pl.loop(1, owners)
-            def _(step):
-                owner = (me + step) % owners
+    def to_owners(send, recv, number, first, some):
+        @pl.loop(0, pairs * some)
+        def _(step):
+            pair = (me // blocks + step // some) % pairs
+            owner = pair * blocks + first + (me + step) % some
+
+            @pl.when(owner != me)
+            def _():
                 remote(send.at[owner], recv.at[me], number, owner, layer)
 
-            local(send.at[me], recv.at[me], number)
-        else:
-            @pl.loop(0, owners)
-            def _(step):
-                owner = (me + step) % owners
-
-                @pl.when(owner != me)
-                def _():
-                    remote(send.at[owner], recv.at[me], number, owner, layer)
-
-                @pl.when(owner == me)
-                def _():
-                    local(send.at[me], recv.at[me], number)
+            @pl.when(owner == me)
+            def _():
+                local(send.at[owner], recv.at[me], number)
 
     def sent_to_owners(send, number):
         if everyone_owns:
@@ -129,11 +122,6 @@
             part()
         else:
             pl.when(me < owners)(part)
-
-    def forward(field):
-        return jnp.dot(field, f_ref[0], preferred_element_type=f32) + jnp.dot(
-            field, f_ref[1], preferred_element_type=f32
-        )
 
     def inverse(value):
         top = value.astype(bf16)
@@ -142,13 +130,28 @@
         both = jnp.dot(jnp.concatenate([top, rest]), i_ref[0], preferred_element_type=f32)
         return (both[:rows] + both[rows:]) + jnp.dot(top, i_ref[1], preferred_element_type=f32)
 
-    def scatter(value, send):
-        for pair in range(pairs):
-            for block in range(blocks):
+    def forward(field, first, last):
+        lanes = slice(first, last)
+        return jnp.dot(field, f_ref[0, :, lanes], preferred_element_type=f32) + jnp.dot(
+            field, f_ref[1, :, lanes], preferred_element_type=f32
+        )
+
+    def transform_out(field, send, recv, number, ready):
+        some = PAIR if blocks % PAIR == 0 else 1
+        for first in range(0, blocks, some):
+            left, right = first * LANES, (first + some) * LANES
+            real = forward(field, left, right)
+            imag = forward(field, half + left, half + right)
+            for pair in range(pairs):
                 rows = slice(pair * 8, pair * 8 + 8)
-                real = value[rows, block * LANES : (block + 1) * LANES]
-                imag = value[rows, half + block * LANES : half + (block + 1) * LANES]
-                send[pair * blocks + block] = jnp.concatenate([real, imag]).astype(bf16)
+                for k in range(some):
+                    lanes = slice(k * LANES, (k + 1) * LANES)
+                    send[pair * blocks + first + k] = jnp.concatenate(
+                        [real[rows, lanes], imag[rows, lanes]]
+                    ).astype(bf16)
+            if first == 0:
+                ready()
+            to_owners(send, recv, number, first, some)
 
     load_k.wait()
 
@@ -215,9 +218,10 @@
     slip_wide = jnp.dot(order, slip_rows.astype(bf16), preferred_element_type=f32)
 
     load_f.wait()
-    scatter(forward(slip_wide.astype(bf16)), send_a)
-    pl.semaphore_wait(barrier, total - 1)
-    to_owners(send_a, recv_a, 0)
+    transform_out(
+        slip_wide.astype(bf16), send_a, recv_a, 0,
+        lambda: pl.semaphore_wait(barrier, total - 1),
+    )
 
     @pl.loop(1, depths)
     def _(step):
@@ -298,8 +302,7 @@
             )
     predicted = inverse(wide[...])
     resid = (weight_wide * (predicted - seen_wide)).astype(bf16)
-    scatter(forward(resid), send_c)
-    to_owners(send_c, recv_c, 2)
+    transform_out(resid, send_c, recv_c, 2, lambda: None)
 
     wide[...] = predicted
     mine = pl.ds(pl.multiple_of(layer * width, LANES), width)
@@ -369,6 +372,19 @@
     @pl.loop(1, depths)
     def _(step):
         wait_bytes(send_o, out_sem.at[4])
+
+
+def hand_over(grad_in, pred_in, grad_out, pred_out, sem):
+    channels = grad_in.shape[2]
+    copies = [
+        pltpu.make_async_copy(grad_in.at[0, 0, c], grad_out.at[0, 0, c], sem.at[c])
+        for c in range(channels)
+    ]
+    copies.append(pltpu.make_async_copy(pred_in, pred_out, sem.at[channels]))
+    for copy in copies:
+        copy.start()
+    for copy in copies:
+        copy.wait()
 
 
 def body(epochs, depths, slip, kernels, lag_index, observed, mask, noise_var, prior_prec):
@@ -385,12 +401,13 @@
     smem = pl.BlockSpec(memory_space=pltpu.SMEM)
     hbm = pl.BlockSpec(memory_space=pltpu.HBM)
     kernels = jnp.swapaxes(kernels, 2, 3)
-    return pl.pallas_call(
+    shapes = (
+        jax.ShapeDtypeStruct(slip.shape, f32),
+        jax.ShapeDtypeStruct(observed.shape, f32),
+    )
+    results = pl.pallas_call(
         functools.partial(kernel, epochs, depths, owners, blocks),
-        out_shape=(
-            jax.ShapeDtypeStruct(slip.shape, f32),
-            jax.ShapeDtypeStruct(observed.shape, f32),
-        ),
+        out_shape=shapes,
         in_specs=[smem, smem, smem, hbm, hbm, hbm, hbm, hbm, hbm],
         out_specs=(vmem, vmem),
         scratch_shapes=[
@@ -426,6 +443,13 @@
         lag_index, noise_var, prior_prec, slip, observed, mask, kernels,
         jnp.asarray(forward_table), jnp.asarray(inverse_table),
     )
+    return pl.pallas_call(
+        hand_over,
+        out_shape=shapes,
+        in_specs=[hbm, hbm],
+        out_specs=(hbm, hbm),
+        scratch_shapes=[pltpu.SemaphoreType.DMA((channels + 1,))],
+    )(*results)
 
 
 def solution(mesh):

time: 32.4 us -> 34.3 us (1.059)
  Pallas kernels: 28 us -> 32.8 us
  local copies, waits for them, and re-layouts: 2.86 us -> 0 us
    pallas_call x0 -> x1, Pallas kernels: none -> 4.61 us  [body(): pl.pallas_call(hand_over, out_shape=shapes, in_specs=[hbm, hbm], out_spec...]
    unnamed x2 -> x0, local copies, waits for them, and re-layouts: 2.86 us -> none
where the time goes in v3:
time: 34.3 us; the launch traced here: 34.1 us
  Pallas kernels  32.8 us (96%)
  between operations  1.29 us (4%)
    pallas_call x1, Pallas kernels, body(): pl.pallas_call(functools.partial(kernel, epochs, depths, owners, blocks),...  28.2 us
    pallas_call x1, Pallas kernels, body(): pl.pallas_call(hand_over, out_shape=shapes, in_specs=[hbm, hbm], out_spec...  4.61 us

profile of v3, /device:TPU:0, one launch (start us, length us, event | category | flops | bytes accessed | tf_op | source)
XLA Modules:
  0.0 34.1 jit_solution(13716784189268317154)
XLA Ops:
  1.3 28.2 %shard_map.104 = (f32[1,1,3,8,1024]{4,3,2,1,0:T(8,128)}, f32[1,8,512]{2,1,0:T(8,128)}) custom-call(s32[16]{0:T(128)} %lag_ref.1, f32[1]{0:T(128)S(6)} %copy.11.nv_ref, f32[1,3]{1,0:T(1,128)} %prior_ref.1, bf16[1,1,3,8,1024]{4,3,2,1,0:T(8,128)(2,1)} %slip_hbm.1, f32[1,8,512]{2,1,0:T(8,128)} %obs_hbm.1, s32[1,8,512]{2,1,0:T(8,128)} %mask_hbm.1, ...), custom_call_target="tpu_custom_call" | custom-call | tf_op jit(solution)/shard_map/pallas_call | solution.py:408
  29.5 4.6 %shard_map.105 = (f32[1,1,3,8,1024]{4,3,2,1,0:T(8,128)}, f32[1,8,512]{2,1,0:T(8,128)}) custom-call(f32[1,1,3,8,1024]{4,3,2,1,0:T(8,128)} %get-tuple-element.4.grad_in, f32[1,8,512]{2,1,0:T(8,128)} %get-tuple-element.5.pred_in), custom_call_target="tpu_custom_call" | custom-call | tf_op jit(solution)/shard_map/pallas_call | solution.py:446

commit v4 on v3

--- a/solution.py
+++ b/solution.py
@@ -374,17 +374,9 @@
         wait_bytes(send_o, out_sem.at[4])
 
 
-def hand_over(grad_in, pred_in, grad_out, pred_out, sem):
-    channels = grad_in.shape[2]
-    copies = [
-        pltpu.make_async_copy(grad_in.at[0, 0, c], grad_out.at[0, 0, c], sem.at[c])
-        for c in range(channels)
-    ]
-    copies.append(pltpu.make_async_copy(pred_in, pred_out, sem.at[channels]))
-    for copy in copies:
-        copy.start()
-    for copy in copies:
-        copy.wait()
+def hand_over(grad_in, pred_in, grad_out, pred_out):
+    grad_out[...] = grad_in[...]
+    pred_out[...] = pred_in[...]
 
 
 def body(epochs, depths, slip, kernels, lag_index, observed, mask, noise_var, prior_prec):
@@ -446,9 +438,8 @@
     return pl.pallas_call(
         hand_over,
         out_shape=shapes,
-        in_specs=[hbm, hbm],
-        out_specs=(hbm, hbm),
-        scratch_shapes=[pltpu.SemaphoreType.DMA((channels + 1,))],
+        in_specs=[vmem, vmem],
+        out_specs=(vmem, vmem),
     )(*results)
 
 

time: 34.3 us -> 31.2 us (0.910)
  Pallas kernels: 32.8 us -> 29.8 us
    pallas_call x1, Pallas kernels: 4.61 us -> 1.55 us  [body(): pl.pallas_call(hand_over, out_shape=shapes, in_specs=[vmem, vmem], out_sp...]
where the time goes in v4:
time: 31.2 us; the launch traced here: 31.1 us
  Pallas kernels  29.8 us (96%)
  between operations  1.29 us (4%)
    pallas_call x1, Pallas kernels, body(): pl.pallas_call(functools.partial(kernel, epochs, depths, owners, blocks),...  28.2 us
    pallas_call x1, Pallas kernels, body(): pl.pallas_call(hand_over, out_shape=shapes, in_specs=[vmem, vmem], out_sp...  1.55 us

profile of v4, /device:TPU:0, one launch (start us, length us, event | category | flops | bytes accessed | tf_op | source)
XLA Modules:
  0.0 31.1 jit_solution(7464060433720218789)
XLA Ops:
  1.3 28.2 %shard_map.104 = (f32[1,1,3,8,1024]{4,3,2,1,0:T(8,128)}, f32[1,8,512]{2,1,0:T(8,128)}) custom-call(s32[16]{0:T(128)} %lag_ref.1, f32[1]{0:T(128)S(6)} %copy.11.nv_ref, f32[1,3]{1,0:T(1,128)} %prior_ref.1, bf16[1,1,3,8,1024]{4,3,2,1,0:T(8,128)(2,1)} %slip_hbm.1, f32[1,8,512]{2,1,0:T(8,128)} %obs_hbm.1, s32[1,8,512]{2,1,0:T(8,128)} %mask_hbm.1, ...), custom_call_target="tpu_custom_call" | custom-call | tf_op jit(solution)/shard_map/pallas_call | solution.py:400
  29.5 1.5 %shard_map.105 = (f32[1,1,3,8,1024]{4,3,2,1,0:T(8,128)}, f32[1,8,512]{2,1,0:T(8,128)}) custom-call(f32[1,1,3,8,1024]{4,3,2,1,0:T(8,128)} %get-tuple-element.4.grad_in, f32[1,8,512]{2,1,0:T(8,128)} %get-tuple-element.5.pred_in), custom_call_target="tpu_custom_call" | custom-call | tf_op jit(solution)/shard_map/pallas_call | solution.py:438
